TPU v7x, 512 devices: a whole 4x8x8 slice. The times are simulated.
512 devices in a mesh: space: 64 (over z, y), tensor: 8 (over x, core).
Axes of the slice: x: 4, y: 8, z: 8, core: 2. Of those that a mesh axis runs over, the one named last changes fastest.
Arguments:
- tokens: bfloat16 [57344, 1024], P('space', 'tensor'), may hold values from -16 to 16
- first_weight: bfloat16 [1024, 1024], P(None, 'tensor'), may hold values from -0.1875 to 0.1875
- second_weight: bfloat16 [1024, 1024], P(None, 'tensor'), may hold values from -0.1875 to 0.1875
- head_weight: bfloat16 [352, 1024], P('tensor'), may hold values from -0.1875 to 0.1875
- targets: float32 [352, 57344], P('tensor', 'space'), may hold values from -6 to 6
- land_mask: int32 [4, 57344], P(None, 'space'), may hold values from 0 to 1, as said below
- variable_kind: int32 [88], P('tensor'), may hold values from 0 to 2
- loss_scale: float32 [], replicated, may hold values from 2523136 to 20185088
Outputs:
- loss: float32 [], replicated
- token_grad: float32 [57344, 1024], P('space', 'tensor')
- first_grad: float32 [1024, 1024], P('space', 'tensor')
- second_grad: float32 [1024, 1024], P('space', 'tensor')
- head_grad: float32 [352, 1024], P('tensor', 'space')
Inputs may be any that keep to these rules, and one draw needn't show every extreme that they name: `land_mask`: every aligned group of 8 entries along the last dimension holds at least one 1 and one 0. `variable_kind`: 0 scores a variable on all cells, 1 on land cells, 2 on ocean cells.
All inputs are finite; a program needn't handle non-finite values.
Results may differ from a plain program's by a relative error of at most 0.0056.
Values may be sent and summed in bfloat16 or wider, within the bound.
No kernel may reach another device: no remote copies, remote signals or barrier semaphores. Data moves between devices by JAX's collectives and lax.ppermute only.
A program may use at most 64 MiB of HBM per device.

v0:
```python
import math
import jax
import jax.numpy as jnp
from jax import lax
from jax.sharding import PartitionSpec as P

V = 88
PP = 4
PROW_DEV = 4
LONP = 224


def sent_to_all(shard, axis):
    copies = jnp.broadcast_to(shard, (lax.axis_size(axis), *shard.shape))
    return lax.all_to_all(copies, axis, split_axis=0, concat_axis=0, tiled=True)


def over_copies(shard, axis):
    everything = sent_to_all(shard, axis)
    return jnp.sum(everything, axis=0)


def split_up(shard, dim, size):
    before, after = (shard.shape[:dim], shard.shape[dim + 1 :])
    return jnp.moveaxis(shard.reshape(*before, size, -1, *after), dim, 0)


def sent_and_summed(shard, axis, dim):
    size = lax.axis_size(axis)
    parts = lax.all_to_all(split_up(shard, dim, size), axis, 0, 0, tiled=True)
    return jnp.sum(parts, axis=0)


def laid_out(parts, dim):
    parts = jnp.moveaxis(parts, 0, dim)
    lengths = parts.shape
    return parts.reshape(*lengths[:dim], lengths[dim] * lengths[dim + 1], *lengths[dim + 2 :])


def gather_directly(shard, axis, dim):
    parts = sent_to_all(shard, axis)
    return laid_out(parts, dim)


def sum_at_owner(shard, axis, dim):
    parts = split_up(shard, dim, lax.axis_size(axis))
    arrived = lax.all_to_all(parts, axis, split_axis=0, concat_axis=0, tiled=True)
    return arrived.astype(jnp.float32).sum(axis=0)


def slope(z):
    cdf = 0.5 * (1.0 + lax.erf(z / math.sqrt(2.0)))
    return cdf + z * jnp.exp(-0.5 * z * z) / math.sqrt(2.0 * math.pi)


def column_folder(weights, piece):
    return lax.dot_general(
        piece, weights, (((1,), (1,)), ((), ())), preferred_element_type=jnp.float32
    )


def row_folder(weights, piece):
    return lax.dot_general(
        piece, weights, (((0,), (0,)), ((), ())), preferred_element_type=jnp.float32
    )


def per_device(
    tokens, first_weight, second_weight, head_weight, targets, land_mask, variable_kind, loss_scale
):
    count = tokens.shape[0]
    width = first_weight.shape[1]
    kinds = head_weight.shape[0] // PP
    rows_first, rows_second = (
        lax.all_to_all(first_weight, "tensor", split_axis=0, concat_axis=1, tiled=True),
        lax.all_to_all(second_weight, "tensor", split_axis=0, concat_axis=1, tiled=True),
    )
    head_cols = lax.all_to_all(head_weight, "tensor", split_axis=1, concat_axis=0, tiled=True)
    position = lax.axis_index("space") * count + jnp.arange(count, dtype=jnp.int32)
    cell = jnp.arange(PP, dtype=jnp.int32)
    lat_row = 2 * (position // LONP)[None, :] + (cell // 2)[:, None]
    nlat = 2 * PROW_DEV * lax.axis_size("space")
    cell_weight = jnp.cos(math.pi / 2.0 * (lat_row.astype(jnp.float32) + 0.5) / nlat)
    land = land_mask.astype(jnp.float32)
    kind = variable_kind[:, None, None]
    valid = jnp.where(kind == 0, 1.0, jnp.where(kind == 1, land[None], 1.0 - land[None]))
    masked = cell_weight[None] * valid
    local_weight = jnp.sum(masked, axis=(1, 2))
    weight_sum = over_copies(local_weight, "space")
    full_in = lax.all_gather(tokens, "tensor", axis=1, tiled=True)
    pre_one = jnp.dot(full_in, first_weight, preferred_element_type=jnp.float32)
    hidden_one = jax.nn.gelu(pre_one, approximate=False).astype(jnp.bfloat16)
    full_one = lax.all_gather(hidden_one, "tensor", axis=1, tiled=True)
    pre_two = jnp.dot(full_one, second_weight, preferred_element_type=jnp.float32)
    hidden_two = jax.nn.gelu(pre_two, approximate=False).astype(jnp.bfloat16)
    full_two = lax.all_gather(hidden_two, "tensor", axis=1, tiled=True)
    predicted = lax.dot_general(
        head_weight, full_two, (((1,), (1,)), ((), ())), preferred_element_type=jnp.float32
    )
    error = predicted.reshape(kinds, PP, count) - targets.reshape(kinds, PP, count)
    local_error = jnp.sum(masked * error * error, axis=(1, 2))
    error_sum = over_copies(local_error, "space")
    root = jnp.sqrt(error_sum / weight_sum + 1e-06)
    loss = lax.psum(jnp.sum(root), "tensor") / V
    coef = loss_scale / (V * root * weight_sum)
    grad_pred = (
        (coef[:, None, None] * masked * error).reshape(kinds * PP, count).astype(jnp.bfloat16)
    )
    back_two = row_folder(head_cols, lax.all_gather(grad_pred, "tensor", axis=0, tiled=True))
    head_term = jnp.dot(grad_pred, full_two, preferred_element_type=jnp.float32)
    head_grad = sent_and_summed(head_term, "space", 1)
    grad_two = (back_two * slope(pre_two)).astype(jnp.bfloat16)
    back_one = column_folder(rows_second, gather_directly(grad_two, "tensor", 1))
    grad_one = (back_one * slope(pre_one)).astype(jnp.bfloat16)
    joined = sum_at_owner(
        jnp.concatenate(
            [
                lax.dot_general(
                    full_one, grad_two, (((0,), (0,)), ((), ())), preferred_element_type=jnp.float32
                ),
                lax.dot_general(
                    full_in, grad_one, (((0,), (0,)), ((), ())), preferred_element_type=jnp.float32
                ),
            ],
            axis=1,
        ).astype(jnp.bfloat16),
        "space",
        0,
    )
    second_grad = joined[:, :width]
    first_grad = joined[:, width:]
    token_grad = column_folder(rows_first, lax.all_gather(grad_one, "tensor", axis=1, tiled=True))
    return (loss, token_grad, first_grad, second_grad, head_grad)


def solution(mesh):
    return jax.shard_map(
        per_device,
        mesh=mesh,
        in_specs=(
            P("space", "tensor"),
            P(None, "tensor"),
            P(None, "tensor"),
            P("tensor", None),
            P("tensor", "space"),
            P(None, "space"),
            P("tensor"),
            P(),
        ),
        out_specs=(
            P(),
            P("space", "tensor"),
            P("space", "tensor"),
            P("space", "tensor"),
            P("tensor", "space"),
        ),
        check_vma=False,
    )
```

profile of v0, /device:TPU:4, one launch (start us, length us, event | category | flops | bytes accessed | tf_op | source)
XLA Modules:
  0.0 263.3 jit_solution(2993436347642144659)
XLA Ops:
  7.2 0.7 all-gather.6.cloned.1.call-update
  7.9 38.0 %all-gather.6.cloned.1.call-done = bf16[896,1024]{1,0:T(8,128)(2,1)} async-done(((bf16[896,128]{1,0:T(8,128)(2,1)}), bf16[896,1024]{1,0:T(8,128)(2,1)}) %all-gather.6.cloned.1.call-update) | async-done | bytes 1835024 | tf_op jit(solution)/shard_map/all_gather | solution.py:90
  46.0 3.6 %fusion.21 = (bf16[896,128]{1,0:T(8,128)(2,1)}, f32[896,128]{1,0:T(8,128)S(1)}) fusion(bf16[896,1024]{1,0:T(8,128)(2,1)} %all-gather.6.cloned.1.call-done, bf16[1024,128]{1,0:T(8,128)(2,1)} %param.9), kind=kOutput, calls=%fused_computation.23 | convolution fusion | flops 242335744 | bytes 2785280 | tf_op jit(solution)/shard_map/dot_general | solution.py:91
  49.7 32.6 %all-gather.8.cloned.1.call-done = bf16[896,1024]{1,0:T(8,128)(2,1)} async-done(((bf16[896,128]{1,0:T(8,128)(2,1)}), bf16[896,1024]{1,0:T(8,128)(2,1)}) %all-gather.8.cloned.1.call-update) | async-done | bytes 1835024 | tf_op jit(solution)/shard_map/all_gather | solution.py:93
  82.3 3.6 %fusion.24 = (bf16[896,128]{1,0:T(8,128)(2,1)}, f32[896,128]{1,0:T(8,128)S(1)}) fusion(bf16[896,1024]{1,0:T(8,128)(2,1)} %all-gather.8.cloned.1.call-done, bf16[1024,128]{1,0:T(8,128)(2,1)} %param.10), kind=kOutput, calls=%fused_computation.26 | convolution fusion | flops 242335744 | bytes 2785280 | tf_op jit(solution)/shard_map/dot_general | solution.py:94
  86.0 0.2 multiply_cosine_fusion
  86.2 0.3 multiply_reduce_fusion
  86.5 0.6 broadcast_in_dim.85
  87.1 13.3 %all-to-all-start.1 = ((f32[64,1,11]{2,1,0:T(1,128)}), f32[64,1,11]{2,1,0:T(1,128)S(1)}, u32[]{:S(2)}, u32[]{:S(2)}) async-start(f32[64,1,11]{2,1,0:T(1,128)} %broadcast_in_dim.85), calls=%async_computation.1 | async-start | bytes 65536 | tf_op jit(solution)/shard_map/all_to_all | solution.py:15
  100.8 0.7 copy.46
  101.7 10.7 %all-to-all-done.1 = f32[64,1,11]{2,1,0:T(1,128)S(1)} async-done(((f32[64,1,11]{2,1,0:T(1,128)}), f32[64,1,11]{2,1,0:T(1,128)S(1)}, u32[]{:S(2)}, u32[]{:S(2)}) %all-to-all-start.1) | async-done | bytes 2848 | tf_op jit(solution)/shard_map/all_to_all | solution.py:15
  112.4 4.8 %all-to-all-start.2 = ((bf16[44,8,128]{2,0,1:T(8,128)(2,1)}), bf16[44,8,128]{2,0,1:T(8,128)(2,1)S(1)}, u32[]{:S(2)}, u32[]{:S(2)}) async-start(bf16[44,8,128]{2,0,1:T(8,128)(2,1)} %copy.46), calls=%async_computation.2 | async-start | bytes 196608 | tf_op jit(solution)/shard_map/all_to_all | solution.py:78
  117.2 1.4 all-gather.10.cloned.1.call-done
  118.6 2.3 fusion.48
  120.9 0.1 reduce_sum.72
  121.1 0.6 broadcast_in_dim.81
  121.7 13.9 %all-to-all-start = ((f32[64,1,11]{2,1,0:T(1,128)}), f32[64,1,11]{2,1,0:T(1,128)S(1)}, u32[]{:S(2)}, u32[]{:S(2)}) async-start(f32[64,1,11]{2,1,0:T(1,128)} %broadcast_in_dim.81), calls=%async_computation | async-start | bytes 65536 | tf_op jit(solution)/shard_map/all_to_all | solution.py:15
  136.4 11.2 %all-to-all-done = f32[64,1,11]{2,1,0:T(1,128)S(1)} async-done(((f32[64,1,11]{2,1,0:T(1,128)}), f32[64,1,11]{2,1,0:T(1,128)S(1)}, u32[]{:S(2)}, u32[]{:S(2)}) %all-to-all-start) | async-done | bytes 2848 | tf_op jit(solution)/shard_map/all_to_all | solution.py:15
  147.5 4.9 %all-to-all-start.4 = ((bf16[8,128,128]{2,1,0:T(8,128)(2,1)}), bf16[8,128,128]{2,1,0:T(8,128)(2,1)S(1)}, u32[]{:S(2)}, u32[]{:S(2)}) async-start(bf16[8,128,128]{2,1,0:T(8,128)(2,1)} %bitcast.4), calls=%async_computation.4 | async-start | bytes 524288 | tf_op jit(solution)/shard_map/all_to_all | solution.py:76
  152.6 0.1 multiply_convert_fusion
  152.8 13.1 %all-gather = bf16[8,44,896]{2,1,0:T(8,128)(2,1)S(1)} all-gather(bf16[1,44,896]{2,1,0:T(8,128)(2,1)S(1)} %bitcast.69), channel_id=1, replica_groups=mesh['space'=64,'tensor'=8] {'tensor'}, dimensions={0}, use_global_device_ids=true | all-gather | bytes 709632 | tf_op jit(solution)/shard_map/all_gather | solution.py:109
  165.9 0.1 reshape.126
  166.0 0.4 fusion.16
  166.4 0.2 broadcast_in_dim.86
  166.7 26.1 %all_to_all.81 = bf16[8,896,128]{2,1,0:T(8,128)(2,1)S(1)} all-to-all(bf16[8,896,128]{2,1,0:T(8,128)(2,1)S(1)} %broadcast_in_dim.86), channel_id=1, replica_groups=mesh['space'=64,'tensor'=8] {'tensor'}, dimensions={0} | all-to-all | bytes 3670016 | tf_op jit(solution)/shard_map/all_to_all | solution.py:15
  192.8 1.3 fusion.13
  194.1 6.5 %all-to-all-start.5 = ((bf16[8,128,128]{2,1,0:T(8,128)(2,1)}), bf16[8,128,128]{2,1,0:T(8,128)(2,1)S(1)}, u32[]{:S(2)}, u32[]{:S(2)}) async-start(bf16[8,128,128]{2,1,0:T(8,128)(2,1)} %bitcast.7), calls=%async_computation.5 | async-start | bytes 524288 | tf_op jit(solution)/shard_map/all_to_all | solution.py:75
  200.6 2.5 copy.49
  203.1 2.6 fusion.7
  205.7 0.3 copy.51
  206.1 1.2 reshape.129
  207.3 2.2 convolution_convert_fusion.1
  209.5 4.8 %all-to-all-start.7 = ((f32[64,1,704]{2,1,0:T(1,128)}), f32[64,1,704]{2,1,0:T(1,128)S(1)}, u32[]{:S(2)}, u32[]{:S(2)}) async-start(f32[64,1,704]{2,1,0:T(1,128)} %reshape.129), calls=%async_computation.7 | async-start | bytes 393216 | tf_op jit(solution)/shard_map/all_to_all | solution.py:30
  214.3 0.5 fusion.17
  214.8 0.2 copy.48
  215.0 0.9 pad_maximum_fusion
  215.8 12.9 %all-to-all-done.7 = f32[64,1,704]{2,1,0:T(1,128)S(1)} async-done(((f32[64,1,704]{2,1,0:T(1,128)}), f32[64,1,704]{2,1,0:T(1,128)S(1)}, u32[]{:S(2)}, u32[]{:S(2)}) %all-to-all-start.7) | async-done | bytes 180256 | tf_op jit(solution)/shard_map/all_to_all | solution.py:30
  228.7 4.6 %all-to-all-start.6 = ((bf16[64,16,256]{2,1,0:T(8,128)(2,1)}), bf16[64,16,256]{2,1,0:T(8,128)(2,1)S(1)}, u32[]{:S(2)}, u32[]{:S(2)}) async-start(bf16[64,16,256]{2,1,0:T(8,128)(2,1)} %pad_maximum_fusion), calls=%async_computation.6 | async-start | bytes 1048576 | tf_op jit(solution)/shard_map/all_to_all | solution.py:47
  233.3 0.6 reduce_sum.76
  233.9 0.2 copy.47
  234.1 11.2 %psum.7 = f32[]{:T(128)} all-reduce(f32[]{:T(128)} %reduce_sum.76), channel_id=1, replica_groups=mesh['space'=64,'tensor'=8] {'tensor'}, use_global_device_ids=true, to_apply=%region_6.7 | all-reduce | flops 1 | bytes 8 | tf_op jit(solution)/shard_map/psum | solution.py:104
  246.0 0.5 broadcast.367
  246.5 1.1 reduce.4
  247.6 0.4 reshape.130
  248.0 0.7 bitcast_reduce_fusion
  248.7 3.3 %all-to-all-done.6 = bf16[64,16,256]{2,1,0:T(8,128)(2,1)S(1)} async-done(((bf16[64,16,256]{2,1,0:T(8,128)(2,1)}), bf16[64,16,256]{2,1,0:T(8,128)(2,1)S(1)}, u32[]{:S(2)}, u32[]{:S(2)}) %all-to-all-start.6) | async-done | bytes 524320 | tf_op jit(solution)/shard_map/all_to_all | solution.py:47
  252.1 0.6 fusion.52
  252.7 2.9 %fusion.53 = f32[896,128]{1,0:T(8,128)} fusion(bf16[896,1024]{1,0:T(8,128)(2,1)} %all-gather.12.cloned.1.call-done, bf16[128,1024]{0,1:T(8,128)(2,1)S(1)} %bitcast.62), kind=kOutput, calls=%fused_computation.90 | convolution fusion | flops 234881024 | bytes 2555904 | tf_op jit(solution)/shard_map/dot_general | solution.py:57
  (49 shorter events, 1.4 us)
Async XLA Ops:
  7.2 38.8 %all-gather.6.cloned.1.call-start = ((), (), s32[]{:S(2)}) async-start(), calls=%async_computation.8 | async-start | bytes 2064384 | tf_op jit(solution)/shard_map/all_gather | solution.py:90
  7.9 74.4 %all-gather.8.cloned.1.call-start = ((), (), s32[]{:S(2)}) async-start(), calls=%async_computation.9 | async-start | bytes 2064384 | tf_op jit(solution)/shard_map/all_gather | solution.py:93
  49.6 36.3 %copy-start.5 = (s32[4,896]{1,0:T(4,128)S(1)}, s32[4,896]{1,0:T(4,128)}, u32[]{:S(2)}) copy-start(s32[4,896]{1,0:T(4,128)} %param.13) | copy-start | bytes 43012
  49.6 36.4 %copy-start.6 = (s32[11]{0:T(128)S(1)}, s32[11]{0:T(128)}, u32[]{:S(2)}) copy-start(s32[11]{0:T(128)} %param.14) | copy-start | bytes 136
  49.6 51.1 %copy-start.3 = (bf16[44,1024]{1,0:T(8,128)(2,1)S(1)}, bf16[44,1024]{1,0:T(8,128)(2,1)}, u32[]{:S(2)}) copy-start(bf16[44,1024]{1,0:T(8,128)(2,1)} %param.11) | copy-start | bytes 270340
  49.6 68.9 %all-gather.10.cloned.1.call-start = ((), (), s32[]{:S(2)}) async-start(), calls=%async_computation.10 | async-start | bytes 2064384 | tf_op jit(solution)/shard_map/all_gather | solution.py:96
  85.9 32.7 %copy-start.4 = (f32[44,896]{1,0:T(8,128)S(1)}, f32[44,896]{1,0:T(8,128)}, u32[]{:S(2)}) copy-start(f32[44,896]{1,0:T(8,128)} %param.12) | copy-start | bytes 473092
  87.1 25.3 %all-to-all-start.1 = ((f32[64,1,11]{2,1,0:T(1,128)}), f32[64,1,11]{2,1,0:T(1,128)S(1)}, u32[]{:S(2)}, u32[]{:S(2)}) async-start(f32[64,1,11]{2,1,0:T(1,128)} %broadcast_in_dim.85), calls=%async_computation.1 | async-start | bytes 65536 | tf_op jit(solution)/shard_map/all_to_all | solution.py:15
  112.4 8.7 %all-to-all-start.2 = ((bf16[44,8,128]{2,0,1:T(8,128)(2,1)}), bf16[44,8,128]{2,0,1:T(8,128)(2,1)S(1)}, u32[]{:S(2)}, u32[]{:S(2)}) async-start(bf16[44,8,128]{2,0,1:T(8,128)(2,1)} %copy.46), calls=%async_computation.2 | async-start | bytes 196608 | tf_op jit(solution)/shard_map/all_to_all | solution.py:78
  121.7 25.8 %all-to-all-start = ((f32[64,1,11]{2,1,0:T(1,128)}), f32[64,1,11]{2,1,0:T(1,128)S(1)}, u32[]{:S(2)}, u32[]{:S(2)}) async-start(f32[64,1,11]{2,1,0:T(1,128)} %broadcast_in_dim.81), calls=%async_computation | async-start | bytes 65536 | tf_op jit(solution)/shard_map/all_to_all | solution.py:15
  147.5 18.9 %all-to-all-start.4 = ((bf16[8,128,128]{2,1,0:T(8,128)(2,1)}), bf16[8,128,128]{2,1,0:T(8,128)(2,1)S(1)}, u32[]{:S(2)}, u32[]{:S(2)}) async-start(bf16[8,128,128]{2,1,0:T(8,128)(2,1)} %bitcast.4), calls=%async_computation.4 | async-start | bytes 524288 | tf_op jit(solution)/shard_map/all_to_all | solution.py:76
  152.4 100.3 %all-gather.12.cloned.1.call-start = ((), (), s32[]{:S(2)}) async-start(), calls=%async_computation.11 | async-start | bytes 2064384 | tf_op jit(solution)/shard_map/all_gather | solution.py:132
  192.8 7.9 %copy-start = (bf16[896,1024]{1,0:T(8,128)(2,1)S(1)}, bf16[896,1024]{1,0:T(8,128)(2,1)}, u32[]{:S(2)}) copy-start(bf16[896,1024]{1,0:T(8,128)(2,1)} %all-gather.10.cloned.1.call-done) | copy-start | bytes 5505028
  194.1 15.4 %all-to-all-start.5 = ((bf16[8,128,128]{2,1,0:T(8,128)(2,1)}), bf16[8,128,128]{2,1,0:T(8,128)(2,1)S(1)}, u32[]{:S(2)}, u32[]{:S(2)}) async-start(bf16[8,128,128]{2,1,0:T(8,128)(2,1)} %bitcast.7), calls=%async_computation.5 | async-start | bytes 524288 | tf_op jit(solution)/shard_map/all_to_all | solution.py:75
  206.0 8.3 %copy-start.1 = (bf16[896,1024]{1,0:T(8,128)(2,1)S(1)}, bf16[896,1024]{1,0:T(8,128)(2,1)}, u32[]{:S(2)}) copy-start(bf16[896,1024]{1,0:T(8,128)(2,1)} %all-gather.6.cloned.1.call-done) | copy-start | bytes 5505028
  206.1 8.3 %copy-start.2 = (bf16[896,128]{1,0:T(8,128)(2,1)S(1)}, bf16[896,128]{1,0:T(8,128)(2,1)}, u32[]{:S(2)}) copy-start(bf16[896,128]{1,0:T(8,128)(2,1)} %fusion.13) | copy-start | bytes 688132
  209.5 19.2 %all-to-all-start.7 = ((f32[64,1,704]{2,1,0:T(1,128)}), f32[64,1,704]{2,1,0:T(1,128)S(1)}, u32[]{:S(2)}, u32[]{:S(2)}) async-start(f32[64,1,704]{2,1,0:T(1,128)} %reshape.129), calls=%async_computation.7 | async-start | bytes 393216 | tf_op jit(solution)/shard_map/all_to_all | solution.py:30
  228.7 23.3 %all-to-all-start.6 = ((bf16[64,16,256]{2,1,0:T(8,128)(2,1)}), bf16[64,16,256]{2,1,0:T(8,128)(2,1)S(1)}, u32[]{:S(2)}, u32[]{:S(2)}) async-start(bf16[64,16,256]{2,1,0:T(8,128)(2,1)} %pad_maximum_fusion), calls=%async_computation.6 | async-start | bytes 1048576 | tf_op jit(solution)/shard_map/all_to_all | solution.py:47
Sparse Core Ops, SparseCore 0:
  10.1 35.7 all-gather.5
  49.7 32.4 all-gather.7
  86.0 32.4 all-gather.9
  194.2 25.7 all-gather.11
where the time goes:
time: 264 us; the launch traced here: 263 us
  waiting for transfers between devices  111 us (42%)
  starting transfers between devices  52.9 us (20%)
  blocking collectives  50.4 us (19%)
  matrix products  19.4 us (7%)
  between operations  16.5 us (6%)
  local copies, waits for them, and re-layouts  9 us (3%)
  other arithmetic  4.24 us (2%)
    all_gather x1, waiting for transfers between devices, per_device(): full_in = lax.all_gather(tokens, 'tensor', axis=1, tiled=True)  38 us
    all_gather x1, waiting for transfers between devices, per_device(): full_one = lax.all_gather(hidden_one, 'tensor', axis=1, tiled=True)  32.6 us
    all_to_all x2, starting transfers between devices, sent_to_all(): return lax.all_to_all(copies, axis, split_axis=0, concat_axis=0, tiled=True)  27.2 us
    all_to_all x1, blocking collectives, sent_to_all(): return lax.all_to_all(copies, axis, split_axis=0, concat_axis=0, tiled=True)  26.1 us
    all_to_all x2, waiting for transfers between devices, sent_to_all(): return lax.all_to_all(copies, axis, split_axis=0, concat_axis=0, tiled=True)  21.8 us
    all_gather x1, blocking collectives, per_device(): lax.all_gather(grad_pred, 'tensor', axis=0, tiled=True)  13.1 us
    all_to_all x1, waiting for transfers between devices, sent_and_summed(): parts = lax.all_to_all(split_up(shard, dim, size), axis, 0, 0, tiled=True)  12.9 us
    psum x1, blocking collectives, per_device(): loss = lax.psum(jnp.sum(root), 'tensor') / V  11.2 us
  transfers between devices with their start and end apart: 11, of which 7 were waited for; matrix products, arithmetic and copies ran while one was open for 8% of the time, Pallas kernels for 0%

commit v1 on v0

--- a/solution.py
+++ b/solution.py
@@ -75,7 +75,9 @@
         lax.all_to_all(first_weight, "tensor", split_axis=0, concat_axis=1, tiled=True),
         lax.all_to_all(second_weight, "tensor", split_axis=0, concat_axis=1, tiled=True),
     )
-    head_cols = lax.all_to_all(head_weight, "tensor", split_axis=1, concat_axis=0, tiled=True)
+    pieces = jnp.split(head_weight, lax.axis_size("tensor"), axis=1)
+    arrived_2 = lax.all_to_all(jnp.stack(pieces), "tensor", 0, 0)
+    head_cols = jnp.concatenate(arrived_2, axis=0)
     position = lax.axis_index("space") * count + jnp.arange(count, dtype=jnp.int32)
     cell = jnp.arange(PP, dtype=jnp.int32)
     lat_row = 2 * (position // LONP)[None, :] + (cell // 2)[:, None]

time: 264 us -> 264 us (level)
  the two profiles are of different devices: /device:TPU:4 before, /device:TPU:2 now
where the time goes in v1:
time: 264 us; the launch traced here: 263 us
  waiting for transfers between devices  107 us (41%)
  blocking collectives  52.2 us (20%)
  starting transfers between devices  51.1 us (19%)
  matrix products  19.4 us (7%)
  between operations  16.5 us (6%)
  local copies, waits for them, and re-layouts  13.1 us (5%)
  other arithmetic  4.24 us (2%)
    all_gather x1, waiting for transfers between devices, per_device(): full_in = lax.all_gather(tokens, 'tensor', axis=1, tiled=True)  37.8 us
    all_gather x1, waiting for transfers between devices, per_device(): full_one = lax.all_gather(hidden_one, 'tensor', axis=1, tiled=True)  32.6 us
    all_to_all x1, blocking collectives, sent_to_all(): return lax.all_to_all(copies, axis, split_axis=0, concat_axis=0, tiled=True)  27.5 us
    all_to_all x2, starting transfers between devices, sent_to_all(): return lax.all_to_all(copies, axis, split_axis=0, concat_axis=0, tiled=True)  25.9 us
    all_to_all x2, waiting for transfers between devices, sent_to_all(): return lax.all_to_all(copies, axis, split_axis=0, concat_axis=0, tiled=True)  17.7 us
    all_gather x1, blocking collectives, per_device(): lax.all_gather(grad_pred, 'tensor', axis=0, tiled=True)  13.4 us
    all_to_all x1, waiting for transfers between devices, sent_and_summed(): parts = lax.all_to_all(split_up(shard, dim, size), axis, 0, 0, tiled=True)  12.9 us
    psum x1, blocking collectives, per_device(): loss = lax.psum(jnp.sum(root), 'tensor') / V  11.2 us
  transfers between devices with their start and end apart: 11, of which 8 were waited for; matrix products, arithmetic and copies ran while one was open for 9% of the time, Pallas kernels for 0%

profile of v1, /device:TPU:2, one launch (start us, length us, event | category | flops | bytes accessed | tf_op | source)
XLA Modules:
  0.0 263.3 jit_solution(7427000295795546951)
XLA Ops:
  7.2 0.7 all-gather.6.cloned.1.call-update
  7.9 37.8 %all-gather.6.cloned.1.call-done = bf16[896,1024]{1,0:T(8,128)(2,1)} async-done(((bf16[896,128]{1,0:T(8,128)(2,1)}), bf16[896,1024]{1,0:T(8,128)(2,1)}) %all-gather.6.cloned.1.call-update) | async-done | bytes 1835024 | tf_op jit(solution)/shard_map/all_gather | solution.py:92
  45.7 3.6 %fusion.21 = (bf16[896,128]{1,0:T(8,128)(2,1)}, f32[896,128]{1,0:T(8,128)S(1)}) fusion(bf16[896,1024]{1,0:T(8,128)(2,1)} %all-gather.6.cloned.1.call-done, bf16[1024,128]{1,0:T(8,128)(2,1)} %param.9), kind=kOutput, calls=%fused_computation.23 | convolution fusion | flops 242335744 | bytes 2785280 | tf_op jit(solution)/shard_map/dot_general | solution.py:93
  49.5 32.6 %all-gather.8.cloned.1.call-done = bf16[896,1024]{1,0:T(8,128)(2,1)} async-done(((bf16[896,128]{1,0:T(8,128)(2,1)}), bf16[896,1024]{1,0:T(8,128)(2,1)}) %all-gather.8.cloned.1.call-update) | async-done | bytes 1835024 | tf_op jit(solution)/shard_map/all_gather | solution.py:95
  82.0 3.6 %fusion.24 = (bf16[896,128]{1,0:T(8,128)(2,1)}, f32[896,128]{1,0:T(8,128)S(1)}) fusion(bf16[896,1024]{1,0:T(8,128)(2,1)} %all-gather.8.cloned.1.call-done, bf16[1024,128]{1,0:T(8,128)(2,1)} %param.10), kind=kOutput, calls=%fused_computation.26 | convolution fusion | flops 242335744 | bytes 2785280 | tf_op jit(solution)/shard_map/dot_general | solution.py:96
  86.2 0.6 broadcast_in_dim.85
  86.9 13.3 %all-to-all-start.1 = ((f32[64,1,11]{2,1,0:T(1,128)}), f32[64,1,11]{2,1,0:T(1,128)S(1)}, u32[]{:S(2)}, u32[]{:S(2)}) async-start(f32[64,1,11]{2,1,0:T(1,128)} %broadcast_in_dim.85), calls=%async_computation.1 | async-start | bytes 65536 | tf_op jit(solution)/shard_map/all_to_all | solution.py:15
  100.2 0.6 constant_dynamic-update-slice_fusion.7
  100.8 0.6 constant_dynamic-update-slice_fusion.6
  101.4 0.6 constant_dynamic-update-slice_fusion.5
  102.0 0.6 constant_dynamic-update-slice_fusion.4
  102.6 0.6 constant_dynamic-update-slice_fusion.3
  103.2 0.6 constant_dynamic-update-slice_fusion.2
  103.8 0.6 constant_dynamic-update-slice_fusion.1
  104.4 0.6 constant_dynamic-update-slice_fusion
  105.6 6.5 %all-to-all-done.1 = f32[64,1,11]{2,1,0:T(1,128)S(1)} async-done(((f32[64,1,11]{2,1,0:T(1,128)}), f32[64,1,11]{2,1,0:T(1,128)S(1)}, u32[]{:S(2)}, u32[]{:S(2)}) %all-to-all-start.1) | async-done | bytes 2848 | tf_op jit(solution)/shard_map/all_to_all | solution.py:15
  112.1 5.1 %all-to-all-start.2 = ((bf16[8,44,128]{2,1,0:T(8,128)(2,1)}), bf16[8,44,128]{2,1,0:T(8,128)(2,1)S(1)}, u32[]{:S(2)}, u32[]{:S(2)}) async-start(bf16[8,44,128]{2,1,0:T(8,128)(2,1)} %constant_dynamic-update-slice_fusion), calls=%async_computation.2 | async-start | bytes 196608 | tf_op jit(solution)/shard_map/all_to_all | solution.py:79
  117.2 1.2 all-gather.10.cloned.1.call-done
  118.4 2.3 fusion.48
  120.8 0.7 all-to-all-done.2
  121.5 0.6 broadcast_in_dim.81
  122.2 12.6 %all-to-all-start = ((f32[64,1,11]{2,1,0:T(1,128)}), f32[64,1,11]{2,1,0:T(1,128)S(1)}, u32[]{:S(2)}, u32[]{:S(2)}) async-start(f32[64,1,11]{2,1,0:T(1,128)} %broadcast_in_dim.81), calls=%async_computation | async-start | bytes 65536 | tf_op jit(solution)/shard_map/all_to_all | solution.py:15
  135.5 11.2 %all-to-all-done = f32[64,1,11]{2,1,0:T(1,128)S(1)} async-done(((f32[64,1,11]{2,1,0:T(1,128)}), f32[64,1,11]{2,1,0:T(1,128)S(1)}, u32[]{:S(2)}, u32[]{:S(2)}) %all-to-all-start) | async-done | bytes 2848 | tf_op jit(solution)/shard_map/all_to_all | solution.py:15
  146.7 5.8 %all-to-all-start.4 = ((bf16[8,128,128]{2,1,0:T(8,128)(2,1)}), bf16[8,128,128]{2,1,0:T(8,128)(2,1)S(1)}, u32[]{:S(2)}, u32[]{:S(2)}) async-start(bf16[8,128,128]{2,1,0:T(8,128)(2,1)} %bitcast.11), calls=%async_computation.4 | async-start | bytes 524288 | tf_op jit(solution)/shard_map/all_to_all | solution.py:76
  152.9 13.4 %all-gather = bf16[8,44,896]{2,1,0:T(8,128)(2,1)S(1)} all-gather(bf16[1,44,896]{2,1,0:T(8,128)(2,1)S(1)} %bitcast.78), channel_id=1, replica_groups=mesh['space'=64,'tensor'=8] {'tensor'}, dimensions={0}, use_global_device_ids=true | all-gather | bytes 709632 | tf_op jit(solution)/shard_map/all_gather | solution.py:111
  166.4 0.4 fusion.16
  167.1 27.5 %all_to_all.67 = bf16[8,896,128]{2,1,0:T(8,128)(2,1)S(1)} all-to-all(bf16[8,896,128]{2,1,0:T(8,128)(2,1)S(1)} %broadcast_in_dim.86), channel_id=1, replica_groups=mesh['space'=64,'tensor'=8] {'tensor'}, dimensions={0} | all-to-all | bytes 3670016 | tf_op jit(solution)/shard_map/all_to_all | solution.py:15
  194.6 1.3 fusion.13
  195.9 4.8 %all-to-all-start.5 = ((bf16[8,128,128]{2,1,0:T(8,128)(2,1)}), bf16[8,128,128]{2,1,0:T(8,128)(2,1)S(1)}, u32[]{:S(2)}, u32[]{:S(2)}) async-start(bf16[8,128,128]{2,1,0:T(8,128)(2,1)} %bitcast.14), calls=%async_computation.5 | async-start | bytes 524288 | tf_op jit(solution)/shard_map/all_to_all | solution.py:75
  200.7 2.5 copy.43
  203.2 2.6 fusion.7
  205.8 0.3 copy.45
  206.2 1.2 reshape.130
  207.4 2.2 convolution_convert_fusion.1
  209.6 4.8 %all-to-all-start.7 = ((f32[64,1,704]{2,1,0:T(1,128)}), f32[64,1,704]{2,1,0:T(1,128)S(1)}, u32[]{:S(2)}, u32[]{:S(2)}) async-start(f32[64,1,704]{2,1,0:T(1,128)} %reshape.130), calls=%async_computation.7 | async-start | bytes 393216 | tf_op jit(solution)/shard_map/all_to_all | solution.py:30
  214.4 0.5 fusion.17
  215.0 0.9 pad_maximum_fusion
  215.9 12.9 %all-to-all-done.7 = f32[64,1,704]{2,1,0:T(1,128)S(1)} async-done(((f32[64,1,704]{2,1,0:T(1,128)}), f32[64,1,704]{2,1,0:T(1,128)S(1)}, u32[]{:S(2)}, u32[]{:S(2)}) %all-to-all-start.7) | async-done | bytes 180256 | tf_op jit(solution)/shard_map/all_to_all | solution.py:30
  228.8 4.6 %all-to-all-start.6 = ((bf16[64,16,256]{2,1,0:T(8,128)(2,1)}), bf16[64,16,256]{2,1,0:T(8,128)(2,1)S(1)}, u32[]{:S(2)}, u32[]{:S(2)}) async-start(bf16[64,16,256]{2,1,0:T(8,128)(2,1)} %pad_maximum_fusion), calls=%async_computation.6 | async-start | bytes 1048576 | tf_op jit(solution)/shard_map/all_to_all | solution.py:47
  233.4 0.6 reduce_sum.76
  234.2 11.2 %psum.7 = f32[]{:T(128)} all-reduce(f32[]{:T(128)} %reduce_sum.76), channel_id=1, replica_groups=mesh['space'=64,'tensor'=8] {'tensor'}, use_global_device_ids=true, to_apply=%region_6.7 | all-reduce | flops 1 | bytes 8 | tf_op jit(solution)/shard_map/psum | solution.py:106
  246.1 0.5 broadcast.367
  246.6 1.1 reduce.4
  247.7 0.4 reshape.131
  248.1 0.7 bitcast_reduce_fusion
  248.8 3.2 %all-to-all-done.6 = bf16[64,16,256]{2,1,0:T(8,128)(2,1)S(1)} async-done(((bf16[64,16,256]{2,1,0:T(8,128)(2,1)}), bf16[64,16,256]{2,1,0:T(8,128)(2,1)S(1)}, u32[]{:S(2)}, u32[]{:S(2)}) %all-to-all-start.6) | async-done | bytes 524320 | tf_op jit(solution)/shard_map/all_to_all | solution.py:47
  252.1 0.6 fusion.52
  252.7 2.9 %fusion.53 = f32[896,128]{1,0:T(8,128)} fusion(bf16[896,1024]{1,0:T(8,128)(2,1)} %all-gather.12.cloned.1.call-done, bf16[128,1024]{0,1:T(8,128)(2,1)S(1)} %bitcast.74), kind=kOutput, calls=%fused_computation.98 | convolution fusion | flops 234881024 | bytes 2555904 | tf_op jit(solution)/shard_map/dot_general | solution.py:57
  (54 shorter events, 2.7 us)
Async XLA Ops:
  7.2 38.6 %all-gather.6.cloned.1.call-start = ((), (), s32[]{:S(2)}) async-start(), calls=%async_computation.8 | async-start | bytes 2064384 | tf_op jit(solution)/shard_map/all_gather | solution.py:92
  7.9 74.1 %all-gather.8.cloned.1.call-start = ((), (), s32[]{:S(2)}) async-start(), calls=%async_computation.9 | async-start | bytes 2064384 | tf_op jit(solution)/shard_map/all_gather | solution.py:95
  49.4 36.3 %copy-start.5 = (s32[4,896]{1,0:T(4,128)S(1)}, s32[4,896]{1,0:T(4,128)}, u32[]{:S(2)}) copy-start(s32[4,896]{1,0:T(4,128)} %param.13) | copy-start | bytes 43012
  49.4 36.4 %copy-start.6 = (s32[11]{0:T(128)S(1)}, s32[11]{0:T(128)}, u32[]{:S(2)}) copy-start(s32[11]{0:T(128)} %param.14) | copy-start | bytes 136
  49.4 50.8 %copy-start.3 = (bf16[44,1024]{1,0:T(8,128)(2,1)S(1)}, bf16[44,1024]{1,0:T(8,128)(2,1)}, u32[]{:S(2)}) copy-start(bf16[44,1024]{1,0:T(8,128)(2,1)} %param.11) | copy-start | bytes 270340
  49.4 69.0 %all-gather.10.cloned.1.call-start = ((), (), s32[]{:S(2)}) async-start(), calls=%async_computation.10 | async-start | bytes 2064384 | tf_op jit(solution)/shard_map/all_gather | solution.py:98
  85.7 32.7 %copy-start.4 = (f32[44,896]{1,0:T(8,128)S(1)}, f32[44,896]{1,0:T(8,128)}, u32[]{:S(2)}) copy-start(f32[44,896]{1,0:T(8,128)} %param.12) | copy-start | bytes 473092
  86.9 25.3 %all-to-all-start.1 = ((f32[64,1,11]{2,1,0:T(1,128)}), f32[64,1,11]{2,1,0:T(1,128)S(1)}, u32[]{:S(2)}, u32[]{:S(2)}) async-start(f32[64,1,11]{2,1,0:T(1,128)} %broadcast_in_dim.85), calls=%async_computation.1 | async-start | bytes 65536 | tf_op jit(solution)/shard_map/all_to_all | solution.py:15
  112.1 9.4 %all-to-all-start.2 = ((bf16[8,44,128]{2,1,0:T(8,128)(2,1)}), bf16[8,44,128]{2,1,0:T(8,128)(2,1)S(1)}, u32[]{:S(2)}, u32[]{:S(2)}) async-start(bf16[8,44,128]{2,1,0:T(8,128)(2,1)} %constant_dynamic-update-slice_fusion), calls=%async_computation.2 | async-start | bytes 196608 | tf_op jit(solution)/shard_map/all_to_all | solution.py:79
  122.2 24.5 %all-to-all-start = ((f32[64,1,11]{2,1,0:T(1,128)}), f32[64,1,11]{2,1,0:T(1,128)S(1)}, u32[]{:S(2)}, u32[]{:S(2)}) async-start(f32[64,1,11]{2,1,0:T(1,128)} %broadcast_in_dim.81), calls=%async_computation | async-start | bytes 65536 | tf_op jit(solution)/shard_map/all_to_all | solution.py:15
  146.7 20.1 %all-to-all-start.4 = ((bf16[8,128,128]{2,1,0:T(8,128)(2,1)}), bf16[8,128,128]{2,1,0:T(8,128)(2,1)S(1)}, u32[]{:S(2)}, u32[]{:S(2)}) async-start(bf16[8,128,128]{2,1,0:T(8,128)(2,1)} %bitcast.11), calls=%async_computation.4 | async-start | bytes 524288 | tf_op jit(solution)/shard_map/all_to_all | solution.py:76
  152.5 100.2 %all-gather.12.cloned.1.call-start = ((), (), s32[]{:S(2)}) async-start(), calls=%async_computation.11 | async-start | bytes 2064384 | tf_op jit(solution)/shard_map/all_gather | solution.py:134
  194.6 6.2 %copy-start = (bf16[896,1024]{1,0:T(8,128)(2,1)S(1)}, bf16[896,1024]{1,0:T(8,128)(2,1)}, u32[]{:S(2)}) copy-start(bf16[896,1024]{1,0:T(8,128)(2,1)} %all-gather.10.cloned.1.call-done) | copy-start | bytes 5505028
  195.9 13.6 %all-to-all-start.5 = ((bf16[8,128,128]{2,1,0:T(8,128)(2,1)}), bf16[8,128,128]{2,1,0:T(8,128)(2,1)S(1)}, u32[]{:S(2)}, u32[]{:S(2)}) async-start(bf16[8,128,128]{2,1,0:T(8,128)(2,1)} %bitcast.14), calls=%async_computation.5 | async-start | bytes 524288 | tf_op jit(solution)/shard_map/all_to_all | solution.py:75
  206.1 8.2 %copy-start.1 = (bf16[896,1024]{1,0:T(8,128)(2,1)S(1)}, bf16[896,1024]{1,0:T(8,128)(2,1)}, u32[]{:S(2)}) copy-start(bf16[896,1024]{1,0:T(8,128)(2,1)} %all-gather.6.cloned.1.call-done) | copy-start | bytes 5505028
  206.1 8.2 %copy-start.2 = (bf16[896,128]{1,0:T(8,128)(2,1)S(1)}, bf16[896,128]{1,0:T(8,128)(2,1)}, u32[]{:S(2)}) copy-start(bf16[896,128]{1,0:T(8,128)(2,1)} %fusion.13) | copy-start | bytes 688132
  209.6 19.2 %all-to-all-start.7 = ((f32[64,1,704]{2,1,0:T(1,128)}), f32[64,1,704]{2,1,0:T(1,128)S(1)}, u32[]{:S(2)}, u32[]{:S(2)}) async-start(f32[64,1,704]{2,1,0:T(1,128)} %reshape.130), calls=%async_computation.7 | async-start | bytes 393216 | tf_op jit(solution)/shard_map/all_to_all | solution.py:30
  228.8 23.2 %all-to-all-start.6 = ((bf16[64,16,256]{2,1,0:T(8,128)(2,1)}), bf16[64,16,256]{2,1,0:T(8,128)(2,1)S(1)}, u32[]{:S(2)}, u32[]{:S(2)}) async-start(bf16[64,16,256]{2,1,0:T(8,128)(2,1)} %pad_maximum_fusion), calls=%async_computation.6 | async-start | bytes 1048576 | tf_op jit(solution)/shard_map/all_to_all | solution.py:47
Sparse Core Ops, SparseCore 0:
  10.1 35.5 all-gather.5
  49.5 32.4 all-gather.7
  85.8 32.5 all-gather.9
  196.1 23.8 all-gather.11
